TPU v7x, 32 devices: a whole 2x2x4 slice. The times are simulated.
32 devices in a mesh: groups: 2 (over y), factor: 4 (over z), dp: 2 (over x), query: 2 (over core).
Axes of the slice: x: 2, y: 2, z: 4, core: 2. Of those that a mesh axis runs over, the one named last changes fastest.
Arguments:
- grad_factors: float32 [192, 14336], P(('groups', 'factor'), ('dp', 'query')), parts along dimension 0, may hold values from -6 to 6
- act_factors: float32 [192, 4096], P(('groups', 'dp', 'query'), 'factor'), parts along dimension 0, may hold values from -6 to 6
- seq_ids: int32 [192], P('groups'), parts along dimension 0, may hold values from 0 to 3, never falling along the last dimension, each value on 1 to 48 neighbouring positions
- out_basis: float32 [14336, 14336], P(('dp', 'query'), 'factor'), may hold values from -0.046875 to 0.046875
- in_basis: float32 [4096, 4096], P('factor', ('dp', 'query')), may hold values from -0.09375 to 0.09375
- eigenvalues: float32 [14336, 4096], P('factor', ('dp', 'query')), may hold values from 0.05 to 5
- damping: float32 [1], replicated, may hold values from 0.02 to 0.2
- query_out: float32 [256, 2, 14336], P(('dp', 'query'), None, 'factor'), may hold values from -0.005859375 to 0.005859375
- query_in: float32 [256, 2, 4096], P('factor', None, ('dp', 'query')), may hold values from -0.005859375 to 0.005859375
- query_ids: int32 [256], replicated, may hold values from 0 to 255, each once
Outputs:
- scores: float32 [8, 256], P('groups', ('factor', 'dp', 'query')), parts along dimension 0
There are 2 independent parts, one for each index of `groups`. A program takes and returns all parts, laid end to end along the dimension named above; an argument that names none is the same for every part. Nothing has to cross between parts.
Inputs may be any that keep to these rules, and one draw needn't show every extreme that they name: `seq_ids`: ids never fall along the tokens, and every sequence holds at least one token. `query_ids`: each query appears once.
All inputs are finite; a program needn't handle non-finite values.
Results may differ from a plain program's by a relative error of at most 0.0003.
Values sent between devices are 32-bit elements; how exact they have to be, the bound alone decides.
A program may use at most 384 MiB of HBM per device.

v0:
```python
import jax
import jax.numpy as jnp
from jax import lax
from jax.sharding import PartitionSpec as P

SEQS = 4


def on_device(
    grad_factors,
    act_factors,
    seq_ids,
    out_basis,
    in_basis,
    eigenvalues,
    damping,
    query_out,
    query_in,
    query_ids,
):
    highest = lax.Precision.HIGHEST
    grad_part = jnp.dot(
        lax.all_gather(grad_factors, "factor", axis=0, tiled=True),
        out_basis,
        precision=highest,
        preferred_element_type=jnp.float32,
    )
    query_cols = lax.all_gather(query_in, "factor", axis=0, tiled=True)
    rot_grad = lax.psum(grad_part, ("dp", "query"))
    act_part = jnp.dot(
        lax.all_gather(act_factors, ("dp", "query"), axis=0, tiled=True),
        in_basis,
        precision=highest,
        preferred_element_type=jnp.float32,
    )
    rot_act = lax.psum(act_part, "factor")
    query_rows = lax.all_gather(query_out, ("dp", "query"), axis=0, tiled=True)
    token_count = rot_act.shape[0]
    inner_width = rot_act.shape[1]
    outer_width = rot_grad.shape[1]
    member = (seq_ids[:, None] == jnp.arange(SEQS, dtype=jnp.int32)[None, :]).astype(jnp.float32)
    weighted = (member[:, :, None] * rot_act[:, None, :]).reshape(token_count, SEQS * inner_width)
    grads = lax.dot_general(
        rot_grad,
        weighted,
        (((0,), (0,)), ((), ())),
        precision=highest,
        preferred_element_type=jnp.float32,
    )
    grads = grads.reshape(outer_width, SEQS, inner_width)
    precond = grads / (eigenvalues[:, None, :] + damping[0])
    query_total = query_cols.shape[0] * query_cols.shape[1]
    query_right = query_cols.reshape(query_total, inner_width)
    query_left = query_rows.reshape(query_total, outer_width)
    cross = lax.dot_general(
        precond.reshape(outer_width * SEQS, inner_width),
        query_right,
        (((1,), (1,)), ((), ())),
        precision=highest,
        preferred_element_type=jnp.float32,
    )
    cross = cross.reshape(outer_width, SEQS, query_total)
    partial_scores = jnp.einsum("isk,ki->sk", cross, query_left, precision=highest)
    partial_scores = jnp.sum(
        partial_scores.reshape(SEQS, query_cols.shape[0], query_cols.shape[1]), axis=2
    )
    partial_scores = partial_scores[:, query_ids]
    halfway = lax.psum_scatter(partial_scores, "factor", scatter_dimension=1, tiled=True)
    scores = lax.psum_scatter(halfway, ("dp", "query"), scatter_dimension=1, tiled=True)
    return scores


def solution(mesh):
    placed = (
        P(("groups", "factor"), ("dp", "query")),
        P(("groups", "dp", "query"), "factor"),
        P("groups"),
        P(("dp", "query"), "factor"),
        P("factor", ("dp", "query")),
        P("factor", ("dp", "query")),
        P(),
        P(("dp", "query"), None, "factor"),
        P("factor", None, ("dp", "query")),
        P(),
    )
    return jax.shard_map(
        on_device,
        mesh=mesh,
        in_specs=placed,
        out_specs=P("groups", ("factor", "dp", "query")),
        check_vma=False,
    )
```

profile of v0, /device:TPU:0, one launch (start us, length us, event | category | flops | bytes accessed | tf_op | source)
XLA Modules:
  0.0 490.8 jit_solution(5611090156376875440)
XLA Ops:
  6.5 0.7 all-gather.4.cloned.1.call-update
  7.3 8.1 %all_gather.13 = f32[96,1024]{1,0:T(8,128)S(1)} all-gather(f32[24,1024]{1,0:T(8,128)} %param.11), channel_id=1, replica_groups=mesh['groups'=2,'factor'=4,'dp'=2,'query'=2] {'dp','query'}, dimensions={0}, use_global_device_ids=true | all-gather | bytes 491520 | tf_op jit(solution)/shard_map/all_gather | solution.py:31
  15.4 5.5 %fusion.9 = f32[96,1024]{1,0:T(8,128)} fusion(f32[96,1024]{1,0:T(8,128)S(1)} %all_gather.13, f32[1024,1024]{1,0:T(8,128)} %param.14), kind=kOutput, calls=%fused_computation.16 | convolution fusion | flops 1207959552 | bytes 4980736 | tf_op jit(solution)/shard_map/dot_general | solution.py:30
  21.0 24.5 %all-gather.4.cloned.1.call-done = f32[96,3584]{1,0:T(8,128)} async-done(((f32[24,3584]{1,0:T(8,128)}), f32[96,3584]{1,0:T(8,128)}) %all-gather.4.cloned.1.call-update) | async-done | bytes 1376272 | tf_op jit(solution)/shard_map/all_gather | solution.py:23
  45.5 34.9 %fusion.8 = f32[96,3584]{1,0:T(8,128)} fusion(f32[96,3584]{1,0:T(8,128)} %all-gather.4.cloned.1.call-done, f32[3584,3584]{1,0:T(8,128)} %param.13), kind=kOutput, calls=%fused_computation.15 | convolution fusion | flops 14797504512 | bytes 54132736 | tf_op jit(solution)/shard_map/dot_general | solution.py:22
  80.5 0.5 all-gather.6.cloned.1.call-update
  81.1 0.5 all-gather.8.cloned.1.call-update
  81.6 0.2 reduce-scatter.3.cloned.1.call-start
  81.8 0.1 fusion.7
  82.6 0.6 pad_clamp_fusion
  83.2 13.9 %broadcast_add_fusion = f32[3584,1024]{1,0:T(8,128)} fusion(f32[3584,1024]{1,0:T(8,128)} %param.15, f32[]{:T(128)} %bitcast.35), kind=kLoop, calls=%fused_computation.4 | loop fusion | flops 3670016 | bytes 29360132 | tf_op jit(solution)/shard_map/add | solution.py:51
  97.1 1.3 broadcast_multiply_fusion
  98.4 27.5 %all-reduce.3.cloned.1.call-done = f32[96,3584]{1,0:T(8,128)} async-done(((f32[96,3584]{1,0:T(8,128)}), f32[96,3584]{1,0:T(8,128)}) %all-reduce.3.cloned.1.call-update) | async-done | bytes 1376272 | tf_op jit(solution)/shard_map/psum | solution.py:29
  125.9 52.7 %fusion.3 = f32[3584,4,1024]{2,0,1:T(8,128)} fusion(f32[96,3584]{1,0:T(8,128)} %all-reduce.3.cloned.1.call-done, f32[12,8,4,1024]{3,2,1,0:T(4,128)S(1)} %bitcast.36), kind=kOutput, calls=%fused_computation.5 | convolution fusion | flops 16911433728 | bytes 61669376 | tf_op jit(solution)/shard_map/dot_general | solution.py:43
  178.6 2.8 reshape.57
  181.5 100.0 %fusion = f32[3584,4,512]{2,0,1:T(8,128)} fusion(f32[512,1024,1]{1,0,2:T(8,128)S(1)} %reshape.57, f32[3584,4,1024]{2,0,1:T(8,128)} %fusion.3, f32[3584,1024]{1,0:T(8,128)} %broadcast_add_fusion), kind=kOutput, calls=%fused_computation.1 | convolution fusion | flops 90208993280 | bytes 104857600 | tf_op jit(solution)/shard_map/dot_general | solution.py:55
  281.5 34.8 %copy.19 = f32[3584,4,512]{0,1,2:T(4,128)} copy(f32[3584,4,512]{2,0,1:T(8,128)} %fusion) | data formatting | bytes 58720256 | tf_op jit(solution)/shard_map/dot_general | solution.py:55
  316.3 13.7 %reshape.62 = f32[512,3584,1]{1,2,0:T(1,128)} reshape(f32[256,2,3584]{2,1,0:T(2,128)} %all-gather.8.cloned.1.call-done) | data formatting | bytes 14680064 | tf_op jit(solution)/shard_map/reshape | solution.py:54
  330.1 111.5 %fusion.10 = f32[512,1,4]{2,1,0:T(1,128)S(1)} fusion(f32[3584,4,512]{0,1,2:T(4,128)} %copy.19, f32[512,3584,1]{1,2,0:T(1,128)} %reshape.62), kind=kOutput, calls=%fused_computation.17 | convolution fusion | flops 88080384 | bytes 36708352 | tf_op jit(solution)/shard_map/isk,ki->sk/dot_general | solution.py:63
  441.6 0.3 reduce_sum.9
  441.9 1.5 gather_fusion
  443.4 19.1 %reduce-scatter.3.cloned.1.call-done = f32[4,64]{0,1:T(8,128)} async-done(((f32[4,256]{0,1:T(8,128)}), f32[4,64]{0,1:T(8,128)}) %reduce-scatter.3.cloned.1.call-update) | async-done | bytes 1040 | tf_op jit(solution)/shard_map/reduce_scatter | solution.py:68
  462.5 20.1 %reduce-scatter.5.cloned.1.call-done = f32[4,16]{0,1:T(8,128)} async-done(((f32[4,64]{0,1:T(8,128)}), f32[4,16]{0,1:T(8,128)}) %reduce-scatter.5.cloned.1.call-update) | async-done | bytes 272 | tf_op jit(solution)/shard_map/reduce_scatter | solution.py:69
  482.6 1.3 copy.18
  (18 shorter events, 0.3 us)
Async XLA Ops:
  6.5 38.9 %all-gather.4.cloned.1.call-start = ((), (), s32[]{:S(2)}) async-start(), calls=%async_computation.2 | async-start | bytes 1720320 | tf_op jit(solution)/shard_map/all_gather | solution.py:23
  7.3 89.8 %all-reduce.5.cloned.1.call-start = ((), (), s32[]{:S(2)}) async-start(), calls=%async_computation.4 | async-start | bytes 786432 | tf_op jit(solution)/shard_map/psum | solution.py:36
  20.9 60.9 %copy-start.1 = (s32[96]{0:T(128)S(1)}, s32[96]{0:T(128)}, u32[]{:S(2)}) copy-start(s32[96]{0:T(128)} %param.12) | copy-start | bytes 1156
  21.0 61.6 %copy-start = (s32[256]{0:T(256)S(1)}, s32[256]{0:T(256)}, u32[]{:S(2)}) copy-start(s32[256]{0:T(256)} %param.19) | copy-start | bytes 3076
  21.0 104.9 %all-reduce.3.cloned.1.call-start = ((), (), s32[]{:S(2)}) async-start(), calls=%async_computation.3 | async-start | bytes 2752512 | tf_op jit(solution)/shard_map/psum | solution.py:29
  80.4 98.2 %all-gather.6.cloned.1.call-start = ((), (), s32[]{:S(2)}) async-start(), calls=%async_computation.5 | async-start | bytes 2621440 | tf_op jit(solution)/shard_map/all_gather | solution.py:28
  81.0 235.3 %all-gather.8.cloned.1.call-start = ((), (), s32[]{:S(2)}) async-start(), calls=%async_computation.6 | async-start | bytes 9175040 | tf_op jit(solution)/shard_map/all_gather | solution.py:37
  81.6 380.9 %reduce-scatter.3.cloned.1.call-start = ((), (), s32[]{:S(2)}) async-start(), calls=%async_computation.7 | async-start | bytes 163840 | tf_op jit(solution)/shard_map/reduce_scatter | solution.py:68
  443.4 39.2 %reduce-scatter.5.cloned.1.call-start = ((), (), s32[]{:S(2)}) async-start(), calls=%async_computation.8 | async-start | bytes 40960 | tf_op jit(solution)/shard_map/reduce_scatter | solution.py:69
Sparse Core Ops, SparseCore 0:
  8.9 36.5 all-gather.3
  47.8 36.0 all-reduce.4
  86.4 39.4 all-reduce.2
  127.3 45.9 all-gather.5
  174.8 51.0 all-gather.7
  443.5 18.9 reduce-scatter.2
  465.1 17.5 reduce-scatter.4
where the time goes:
time: 492 us; the launch traced here: 491 us
  matrix products  305 us (62%)
  waiting for transfers between devices  92.9 us (19%)
  local copies, waits for them, and re-layouts  54.2 us (11%)
  other arithmetic  16.2 us (3%)
  between operations  14.2 us (3%)
  blocking collectives  8.12 us (2%)
    dot_general x1, matrix products, on_device(): jnp.einsum('isk,ki->sk', cross, query_left, precision=highest)  112 us
    dot_general x1, matrix products, on_device(): lax.dot_general(precond.reshape(outer_width * SEQS, inner_width), query_r...  100 us
    dot_general x1, matrix products, on_device(): lax.dot_general(rot_grad, weighted, (((0,), (0,)), ((), ())), precision=h...  52.7 us
    dot_general x1, matrix products, on_device(): jnp.dot(lax.all_gather(grad_factors, 'factor', axis=0, tiled=True), out_b...  34.9 us
    dot_general x1, local copies, waits for them, and re-layouts, on_device(): lax.dot_general(precond.reshape(outer_width * SEQS, inner_width), query_r...  34.8 us
    psum x1, waiting for transfers between devices, on_device(): rot_grad = lax.psum(grad_part, ('dp', 'query'))  27.5 us
    all_gather x1, waiting for transfers between devices, on_device(): lax.all_gather(grad_factors, 'factor', axis=0, tiled=True)  24.5 us
    reduce_scatter x1, waiting for transfers between devices, on_device(): lax.psum_scatter(halfway, ('dp', 'query'), scatter_dimension=1, tiled=True)  20.1 us
  transfers between devices with their start and end apart: 7, of which 4 were waited for; matrix products, arithmetic and copies ran while one was open for 50% of the time, Pallas kernels for 0%

commit v1 on v0

v1 whole, which is shorter than its diff:
```python
import functools

import jax
import jax.numpy as jnp
from jax import lax
from jax.experimental import pallas as pl
from jax.experimental.pallas import tpu as pltpu
from jax.sharding import PartitionSpec as P

SEQS = 4
F32 = jnp.float32
BF16 = jnp.bfloat16
VMEM_BYTES = 56 * 1024 * 1024


def tile_of(width, most):
    for tile in range(most, 0, -128):
        if width % tile == 0:
            return tile
    return width


def halves(x):
    high = x.astype(BF16)
    return high, (x - high.astype(F32)).astype(BF16)


def dot(a, b, contract=((1,), (0,))):
    return lax.dot_general(a, b, (contract, ((), ())), preferred_element_type=F32)


def rotate_kernel(x_ref, basis_ref, out_ref, x_both):
    rows = x_ref.shape[0]

    @pl.when(pl.program_id(0) == 0)
    def _():
        high, low = halves(x_ref[...])
        x_both[:rows, :] = high
        x_both[rows:, :] = low

    high, low = halves(basis_ref[...])
    both = dot(x_both[...], high)
    out_ref[...] = both[:rows] + both[rows:] + dot(x_both[:rows, :], low)


def rotate(x, basis, part, parts):
    rows, depth = x.shape
    width = basis.shape[1] // parts
    tile = tile_of(width, 512)
    steps = width // tile
    return pl.pallas_call(
        rotate_kernel,
        grid=(steps,),
        in_specs=[
            pl.BlockSpec((rows, depth), lambda n: (0, 0)),
            pl.BlockSpec((depth, tile), lambda n: (0, part * steps + n)),
        ],
        out_specs=pl.BlockSpec((rows, tile), lambda n: (0, n)),
        out_shape=jax.ShapeDtypeStruct((rows, width), F32),
        scratch_shapes=[pltpu.VMEM((2 * rows, depth), BF16)],
        compiler_params=pltpu.CompilerParams(vmem_limit_bytes=VMEM_BYTES),
        cost_estimate=pl.CostEstimate(
            flops=6 * rows * depth * width, bytes_accessed=4 * depth * width, transcendentals=0
        ),
        name="rotate",
    )(x, basis)


def score_kernel(ids_ref, damping_ref, acts_ref, grads_ref, eig_ref, right_ref, left_ref, out_ref, weighted, right_high, right_low):
    tokens, inner = acts_ref.shape

    @pl.when(pl.program_id(0) == 0)
    def _():
        out_ref[...] = jnp.zeros_like(out_ref)
        for s in range(SEQS):
            member = ids_ref[...] == s
            high, low = halves(jnp.where(member, acts_ref[...], 0.0))
            cols = slice(s * inner, (s + 1) * inner)
            weighted[:tokens, cols] = high
            weighted[tokens : 2 * tokens, cols] = low
            weighted[2 * tokens :, cols] = high
        high, low = halves(right_ref[...].T)
        right_high[...] = high
        right_low[...] = low

    rows = eig_ref.shape[0]
    inverse = 1.0 / (eig_ref[...] + damping_ref[0])
    grad_high, grad_low = halves(grads_ref[...])
    grad_all = jnp.concatenate([grad_high, grad_high, grad_low], axis=0)
    left = left_ref[...].T
    for s in range(SEQS):
        grad_seq = dot(grad_all, weighted[:, s * inner : (s + 1) * inner], ((0,), (0,)))
        high, low = halves(grad_seq * inverse)
        cross = dot(high, right_high[...]) + dot(high, right_low[...]) + dot(low, right_high[...])
        terms = (cross * left).reshape(rows // 8, 8, cross.shape[1])
        out_ref[s * 8 : (s + 1) * 8, :] += jnp.sum(terms, axis=0)


def score(ids, damping, acts, grads, eigenvalues, right, left, part, parts):
    tokens, inner = acts.shape
    queries = right.shape[0]
    outer = eigenvalues.shape[0] // parts
    tile = tile_of(outer, 256)
    steps = outer // tile
    whole = lambda i: (0, 0)
    return pl.pallas_call(
        score_kernel,
        grid=(steps,),
        in_specs=[
            pl.BlockSpec((tokens, 1), whole),
            pl.BlockSpec(memory_space=pltpu.SMEM),
            pl.BlockSpec((tokens, inner), whole),
            pl.BlockSpec((tokens, tile), lambda i: (0, i)),
            pl.BlockSpec((tile, inner), lambda i: (part * steps + i, 0)),
            pl.BlockSpec((queries, inner), whole),
            pl.BlockSpec((queries, tile), lambda i: (0, part * steps + i)),
        ],
        out_specs=pl.BlockSpec((SEQS * 8, queries), whole),
        out_shape=jax.ShapeDtypeStruct((SEQS * 8, queries), F32),
        scratch_shapes=[
            pltpu.VMEM((3 * tokens, SEQS * inner), BF16),
            pltpu.VMEM((inner, queries), BF16),
            pltpu.VMEM((inner, queries), BF16),
        ],
        compiler_params=pltpu.CompilerParams(vmem_limit_bytes=VMEM_BYTES),
        cost_estimate=pl.CostEstimate(
            flops=6 * SEQS * outer * inner * (queries + 2 * tokens),
            bytes_accessed=4 * outer * (inner + queries),
            transcendentals=0,
        ),
        name="score",
    )(ids.reshape(tokens, 1), damping, acts, grads, eigenvalues, right, left)


def swap(x, axis):
    return lax.ppermute(x, axis, [(0, 1), (1, 0)])


def place(blocks, at, count):
    rows = blocks[0].shape[0]
    out = jnp.zeros((rows * count,) + blocks[0].shape[1:], blocks[0].dtype)
    for block, index in zip(blocks, at):
        out = lax.dynamic_update_slice_in_dim(out, block, index * rows, 0)
    return out


def gather_line(x, axis, size):
    me = lax.axis_index(axis)
    blocks, at = [x], [me]
    for shift in range(1, size):
        blocks.append(lax.ppermute(x, axis, [(i, (i + shift) % size) for i in range(size)]))
        at.append(lax.rem(me + size - shift, size))
    return blocks, at


def my_half(x, index, own):
    rows = x.shape[0] // 2
    first, second = x[:rows], x[rows:]
    pick_second = (index == 1) if own else (index == 0)
    return jnp.where(pick_second, second, first)


def join(mine, other, index):
    return jnp.where(index == 0, jnp.concatenate([mine, other]), jnp.concatenate([other, mine]))


def flip(x, axis, size, bit):
    return lax.ppermute(x, axis, [(i, i ^ bit) for i in range(size)])


def sum_line(x, axis, size):
    me = lax.axis_index(axis)
    bits, bit = [], 1
    while bit < size:
        index = lax.rem(me // bit, 2)
        x = my_half(x, index, True) + flip(my_half(x, index, False), axis, size, bit)
        bits.append((bit, index))
        bit *= 2
    for bit, index in reversed(bits):
        x = join(x, flip(x, axis, size, bit), index)
    return x


def scatter_sum(x, axes, sizes):
    for axis, size in zip(axes, sizes):
        me = lax.axis_index(axis)
        bit = size // 2
        while bit:
            upper = lax.rem(me // bit, 2) == 1
            wide = x.shape[1] // 2
            first, second = x[:, :wide], x[:, wide:]
            x = jnp.where(upper, second, first) + flip(jnp.where(upper, first, second), axis, size, bit)
            bit //= 2
    return x


def on_device(
    sizes,
    grad_factors,
    act_factors,
    seq_ids,
    out_basis,
    in_basis,
    eigenvalues,
    damping,
    query_out,
    query_in,
    query_ids,
):
    groups, factor, dp, core = sizes
    small = groups == 2 and factor == 4 and dp == 2 and core == 2
    parts = 2 if small else 1
    flat_out = query_out.reshape(-1, query_out.shape[2])
    flat_in = query_in.reshape(-1, query_in.shape[2])
    if small:
        g = lax.axis_index("groups")
        x = lax.axis_index("dp")
        c = lax.axis_index("query")
        pair = join(act_factors, swap(act_factors, "query"), c)
        acts_all = join(pair, swap(pair, "dp"), x)
        grads_all = place(*gather_line(grad_factors, "factor", factor), factor)
        half_in, at = gather_line(my_half(flat_in, g, True), "factor", factor)
        blocks = [flat_in] + [join(b, swap(b, "groups"), g) for b in half_in[1:]]
        right = place(blocks, at, factor)
        half_out = swap(my_half(flat_out, g, True), "dp")
        other_chip = join(half_out, swap(half_out, "groups"), g)
        own_core = join(flat_out, other_chip, x)
        other_core = swap(own_core, "query")
        rows = flat_out.shape[0]
        low = jnp.where(c == 0, own_core, other_core)
        high = jnp.where(c == 0, other_core, own_core)
        left = jnp.concatenate([low[:rows], high[:rows], low[rows:], high[rows:]])
    else:
        acts_all = lax.all_gather(act_factors, ("dp", "query"), axis=0, tiled=True)
        grads_all = lax.all_gather(grad_factors, "factor", axis=0, tiled=True)
        right = lax.all_gather(flat_in, "factor", axis=0, tiled=True)
        left = lax.all_gather(flat_out, ("dp", "query"), axis=0, tiled=True)

    rot_act = rotate(acts_all, in_basis, 0, 1)
    rot_act = sum_line(rot_act, "factor", factor) if small else lax.psum(rot_act, "factor")

    total = None
    for part in range(parts):
        rot_grad = rotate(grads_all, out_basis, part, parts)
        if small:
            mine = my_half(rot_grad, c, True) + swap(my_half(rot_grad, c, False), "query")
            mine = mine + swap(mine, "dp")
            rot_grad = join(mine, swap(mine, "query"), c)
        else:
            rot_grad = lax.psum(rot_grad, ("dp", "query"))
        one = score(seq_ids, damping, rot_act, rot_grad, eigenvalues, right, left, part, parts)
        total = one if total is None else total + one

    count = query_ids.shape[0]
    raw = jnp.sum(total.reshape(SEQS, 8, count, -1), axis=(1, 3))
    raw = raw[:, query_ids]
    return scatter_sum(raw, ("factor", "dp", "query"), (factor, dp, core))


def solution(mesh):
    sizes = tuple(mesh.shape[a] for a in ("groups", "factor", "dp", "query"))
    placed = (
        P(("groups", "factor"), ("dp", "query")),
        P(("groups", "dp", "query"), "factor"),
        P("groups"),
        P(("dp", "query"), "factor"),
        P("factor", ("dp", "query")),
        P("factor", ("dp", "query")),
        P(),
        P(("dp", "query"), None, "factor"),
        P("factor", None, ("dp", "query")),
        P(),
    )
    return jax.shard_map(
        functools.partial(on_device, sizes),
        mesh=mesh,
        in_specs=placed,
        out_specs=P("groups", ("factor", "dp", "query")),
        check_vma=False,
    )
```

time: 492 us -> 220 us (0.45)
  matrix products: 305 us -> 0 us
  Pallas kernels: 0 us -> 102 us
  waiting for transfers between devices: 92.9 us -> 39.9 us
  starting transfers between devices: 0.42 us -> 41.7 us
  local copies, waits for them, and re-layouts: 54.2 us -> 15.6 us
  between operations: 14.2 us -> 1.13 us
  blocking collectives: 8.12 us -> 0 us
    dot_general x5 -> x0, matrix products: 305 us -> none  [the longest x1 112 us: on_device(): jnp.einsum('isk,ki->sk', cross, query_left, precision=highest)]
    pallas_call x0 -> x5, Pallas kernels: none -> 102 us  [the longest x2 72.2 us: score(): pl.pallas_call(score_kernel, grid=(steps,), in_specs=[pl.BlockSpec((token...]
    ppermute x0 -> x28, starting transfers between devices: none -> 41.7 us  [the longest x8 20.8 us: flip(): return lax.ppermute(x, axis, [(i, i ^ bit) for i in range(size)])]
    ppermute x0 -> x28, waiting for transfers between devices: none -> 39.9 us  [the longest x8 15.1 us: flip(): return lax.ppermute(x, axis, [(i, i ^ bit) for i in range(size)])]
    reduce_scatter x2 -> x0, waiting for transfers between devices: 39.1 us -> none  [the longest x1 20.1 us: on_device(): lax.psum_scatter(halfway, ('dp', 'query'), scatter_dimension=1, tiled=True)]
    dot_general x1 -> x0, local copies, waits for them, and re-layouts: 34.8 us -> none  [on_device(): lax.dot_general(precond.reshape(outer_width * SEQS, inner_width), query_r...]
    psum x2 -> x0, waiting for transfers between devices: 27.5 us -> none  [the longest x1 27.5 us: on_device(): rot_grad = lax.psum(grad_part, ('dp', 'query'))]
    all_gather x3 -> x0, waiting for transfers between devices: 24.5 us -> none  [the longest x1 24.5 us: on_device(): lax.all_gather(grad_factors, 'factor', axis=0, tiled=True)]
  transfers between devices with their start and end apart: 7 -> 28, of which waited for: 4 -> 13; matrix products, arithmetic and copies ran while one was open for 50% -> 11% of each run, Pallas kernels for 0% -> 13%
where the time goes in v1:
time: 220 us; the launch traced here: 219 us
  Pallas kernels  102 us (46%)
  starting transfers between devices  41.7 us (19%)
  waiting for transfers between devices  39.9 us (18%)
  other arithmetic  19.1 us (9%)
  local copies, waits for them, and re-layouts  15.6 us (7%)
    pallas_call x2, Pallas kernels, score(): pl.pallas_call(score_kernel, grid=(steps,), in_specs=[pl.BlockSpec((token...  72.2 us
    pallas_call x3, Pallas kernels, rotate(): pl.pallas_call(rotate_kernel, grid=(steps,), in_specs=[pl.BlockSpec((rows...  29.5 us
    ppermute x8, starting transfers between devices, flip(): return lax.ppermute(x, axis, [(i, i ^ bit) for i in range(size)])  20.8 us
    ppermute x8, waiting for transfers between devices, flip(): return lax.ppermute(x, axis, [(i, i ^ bit) for i in range(size)])  15.1 us
    ppermute x6, waiting for transfers between devices, gather_line(): lax.ppermute(x, axis, [(i, (i + shift) % size) for i in range(size)])  12.8 us
    ppermute x14, waiting for transfers between devices, swap(): return lax.ppermute(x, axis, [(0, 1), (1, 0)])  12 us
    ppermute x6, starting transfers between devices, gather_line(): lax.ppermute(x, axis, [(i, (i + shift) % size) for i in range(size)])  10.5 us
    ppermute x14, starting transfers between devices, swap(): return lax.ppermute(x, axis, [(0, 1), (1, 0)])  10.4 us
  transfers between devices with their start and end apart: 28, of which 13 were waited for; matrix products, arithmetic and copies ran while one was open for 11% of the time, Pallas kernels for 13%

profile of v1, /device:TPU:0, one launch (start us, length us, event | category | flops | bytes accessed | tf_op | source)
XLA Modules:
  0.0 219.2 jit_solution(1309289710468842088)
XLA Ops:
  0.0 3.0 %collective-permute-start.6 = (f32[24,3584]{1,0:T(8,128)}, f32[24,3584]{1,0:T(8,128)}, u32[]{:S(2)}, u32[]{:S(2)}) collective-permute-start(f32[24,3584]{1,0:T(8,128)} %param.10), channel_id=1, source_target_pairs={{0,4},{4,8},{8,12},{12,0},{1,5},{5,9},{9,13},{13,1},{2,6},{6,10},{... | collective-permute-start | bytes 1032200 | tf_op jit(solution)/shard_map/ppermute | solution.py:151
  3.0 2.6 %collective-permute-start.7 = (f32[24,3584]{1,0:T(8,128)}, f32[24,3584]{1,0:T(8,128)}, u32[]{:S(2)}, u32[]{:S(2)}) collective-permute-start(f32[24,3584]{1,0:T(8,128)} %param.10), channel_id=1, source_target_pairs={{0,8},{4,12},{8,0},{12,4},{1,9},{5,13},{9,1},{13,5},{2,10},{6,14},... | collective-permute-start | bytes 1032200 | tf_op jit(solution)/shard_map/ppermute | solution.py:151
  9.6 3.0 %slice_select_fusion = f32[32,2,3584]{2,1,0:T(2,128)} fusion(f32[64,2,3584]{2,1,0:T(2,128)} %param.17, pred[]{:T(512)S(6)} %eq.59), kind=kLoop, calls=%fused_computation.6 | loop fusion | flops 229376 | bytes 2752513 | tf_op jit(solution)/shard_map/jit(_where)/select_n | solution.py:160
  14.0 2.5 %reshape.23 = f32[128,3584]{1,0:T(8,128)} reshape(f32[64,2,3584]{2,1,0:T(2,128)S(1)} %copy-done.1) | data formatting | bytes 3670016 | tf_op jit(solution)/shard_map/reshape | solution.py:213
  24.1 5.5 %collective-permute-done.1 = f32[48,1024]{1,0:T(8,128)S(1)} collective-permute-done((f32[48,1024]{1,0:T(8,128)S(1)}, f32[48,1024]{1,0:T(8,128)S(1)}, u32[]{:S(2)}, u32[]{:S(2)}) %collective-permute-start.1) | collective-permute-done | bytes 196640 | tf_op jit(solution)/shard_map/ppermute | solution.py:136
  31.9 3.6 %rotate.3 = f32[96,1024]{1,0:T(8,128)} custom-call(f32[96,1024]{1,0:T(8,128)} %maximum_select_fusion.7.x_ref, f32[1024,1024]{1,0:T(8,128)} %basis_ref.3), custom_call_target="tpu_custom_call" | custom-call | flops 603979776 | bytes 4194304 | tf_op jit(solution)/shard_map/rotate/pallas_call | solution.py:51
  36.5 2.0 collective-permute-start.16
  40.5 4.6 %collective-permute-done.14 = f32[64,1024]{1,0:T(8,128)} collective-permute-done((f32[64,1024]{1,0:T(8,128)}, f32[64,1024]{1,0:T(8,128)}, u32[]{:S(2)}, u32[]{:S(2)}) %collective-permute-start.14) | collective-permute-done | bytes 262176 | tf_op jit(solution)/shard_map/ppermute | solution.py:151
  46.7 3.9 %collective-permute-done.16 = f32[64,1024]{1,0:T(8,128)S(1)} collective-permute-done((f32[64,1024]{1,0:T(8,128)}, f32[64,1024]{1,0:T(8,128)S(1)}, u32[]{:S(2)}, u32[]{:S(2)}) %collective-permute-start.16) | collective-permute-done | bytes 262176 | tf_op jit(solution)/shard_map/ppermute | solution.py:151
  53.7 4.2 %collective-permute-done.8 = f32[24,3584]{1,0:T(8,128)S(1)} collective-permute-done((f32[24,3584]{1,0:T(8,128)S(1)}, f32[24,3584]{1,0:T(8,128)S(1)}, u32[]{:S(2)}, u32[]{:S(2)}) %collective-permute-start.8) | collective-permute-done | bytes 344096 | tf_op jit(solution)/shard_map/ppermute | solution.py:151
  57.9 3.6 %collective-permute-start.2 = (f32[48,1024]{1,0:T(8,128)S(1)}, f32[48,1024]{1,0:T(8,128)S(1)}, u32[]{:S(2)}, u32[]{:S(2)}) collective-permute-start(f32[48,1024]{1,0:T(8,128)S(1)} %slice_select_fusion.4), channel_id=1, source_target_pairs={{0,4},{4,0},{8,12},{12,8},{1,5},{5,1},{9,13},{13,9},{2,6},{6,2},{1... | collective-permute-start | bytes 589832 | tf_op jit(solution)/shard_map/ppermute | solution.py:168
  63.1 13.0 %rotate.5 = f32[96,1792]{1,0:T(8,128)} custom-call(f32[96,3584]{1,0:T(8,128)} %copy-done, f32[3584,3584]{1,0:T(8,128)} %basis_ref.5), custom_call_target="tpu_custom_call" | custom-call | flops 3699376128 | bytes 25690112 | tf_op jit(solution)/shard_map/rotate/pallas_call | solution.py:51
  76.1 13.0 %rotate.4 = f32[96,1792]{1,0:T(8,128)} custom-call(f32[96,3584]{1,0:T(8,128)} %copy-done, f32[3584,3584]{1,0:T(8,128)} %basis_ref.5), custom_call_target="tpu_custom_call" | custom-call | flops 3699376128 | bytes 25690112 | tf_op jit(solution)/shard_map/rotate/pallas_call | solution.py:51
  92.1 3.4 %collective-permute-start.3 = (f32[24,1024]{1,0:T(8,128)S(1)}, f32[24,1024]{1,0:T(8,128)S(1)}, u32[]{:S(2)}, u32[]{:S(2)}) collective-permute-start(f32[24,1024]{1,0:T(8,128)S(1)} %slice_select_fusion.5), channel_id=1, source_target_pairs={{0,8},{4,12},{8,0},{12,4},{1,9},{5,13},{9,1},{13,5},{2,10},{6,14},... | collective-permute-start | bytes 294920 | tf_op jit(solution)/shard_map/ppermute | solution.py:168
  96.6 2.3 %collective-permute-done.3 = f32[24,1024]{1,0:T(8,128)S(1)} collective-permute-done((f32[24,1024]{1,0:T(8,128)S(1)}, f32[24,1024]{1,0:T(8,128)S(1)}, u32[]{:S(2)}, u32[]{:S(2)}) %collective-permute-start.3) | collective-permute-done | bytes 98336 | tf_op jit(solution)/shard_map/ppermute | solution.py:168
  99.0 2.7 %collective-permute-start.4 = (f32[24,1024]{1,0:T(8,128)S(1)}, f32[24,1024]{1,0:T(8,128)S(1)}, u32[]{:S(2)}, u32[]{:S(2)}) collective-permute-start(f32[24,1024]{1,0:T(8,128)S(1)} %select_add_fusion.3), channel_id=1, source_target_pairs={{0,8},{4,12},{8,0},{12,4},{1,9},{5,13},{9,1},{13,5},{2,10},{6,14},... | collective-permute-start | bytes 294920 | tf_op jit(solution)/shard_map/ppermute | solution.py:168
  106.7 6.0 %collective-permute-done.22 = f32[48,1792]{1,0:T(8,128)S(1)} collective-permute-done((f32[48,1792]{1,0:T(8,128)S(1)}, f32[48,1792]{1,0:T(8,128)S(1)}, u32[]{:S(2)}, u32[]{:S(2)}) %collective-permute-start.22) | collective-permute-done | bytes 344096 | tf_op jit(solution)/shard_map/ppermute | solution.py:136
  112.7 4.8 %collective-permute-start.5 = (f32[48,1024]{1,0:T(8,128)S(1)}, f32[48,1024]{1,0:T(8,128)S(1)}, u32[]{:S(2)}, u32[]{:S(2)}) collective-permute-start(f32[48,1024]{1,0:T(8,128)S(1)} %maximum_select_fusion.10), channel_id=1, source_target_pairs={{0,4},{4,0},{8,12},{12,8},{1,5},{5,1},{9,13},{13,9},{2,6},{6,2},{1... | collective-permute-start | bytes 589832 | tf_op jit(solution)/shard_map/ppermute | solution.py:168
  125.1 3.2 %pad_maximum_fusion.left_ref = f32[512,3584]{1,0:T(8,128)} fusion(f32[128,3584]{1,0:T(8,128)S(1)} %get-tuple-element.11, f32[128,3584]{1,0:T(8,128)S(1)} %get-tuple-element.8, f32[128,3584]{1,0:T(8,128)S(1)} %get-tuple-element.12, f32[128,3584]{1,0:T(8,128)S(1)} %get-tuple-element.7), kind=kLoop, calls=%fused_computation.1 | loop fusion | flops 5505024 | bytes 14680064 | tf_op jit(solution)/shard_map/concatenate | solution.py:232
  128.3 36.0 %score.3 = f32[32,512]{1,0:T(8,128)} custom-call(s32[96,1]{1,0:T(8,128)} %copy.14.ids_ref, f32[1]{0:T(128)S(6)} %copy.26.damping_ref, f32[96,1024]{1,0:T(8,128)} %maximum_select_fusion.8.acts_ref, f32[96,1792]{1,0:T(8,128)} %maximum_select_fusion.3.grads_ref, f32[3584,1024]{1,0:T(8,128)} %eig_ref.3, f32[512,1024]{1,0:T(8,128)} %copy-done.6, ...), custom_call_target="tpu_custom_call" | custom-call | flops 31004295168 | bytes 11010048 | tf_op jit(solution)/shard_map/score/pallas_call | solution.py:106
  164.3 36.2 %score.2 = f32[32,512]{1,0:T(8,128)} custom-call(s32[96,1]{1,0:T(8,128)} %copy.14.ids_ref, f32[1]{0:T(128)S(6)} %copy.26.damping_ref, f32[96,1024]{1,0:T(8,128)} %maximum_select_fusion.8.acts_ref, f32[96,1792]{1,0:T(8,128)} %maximum_select_fusion.2.grads_ref, f32[3584,1024]{1,0:T(8,128)} %eig_ref.3, f32[512,1024]{1,0:T(8,128)} %copy-done.6, ...), custom_call_target="tpu_custom_call" | custom-call | flops 31004295168 | bytes 11010048 | tf_op jit(solution)/shard_map/score/pallas_call | solution.py:106
  204.4 3.9 %collective-permute-done.24 = f32[4,128]{0,1:T(8,128)S(1)} collective-permute-done((f32[4,128]{0,1:T(8,128)S(1)}, f32[4,128]{0,1:T(8,128)S(1)}, u32[]{:S(2)}, u32[]{:S(2)}) %collective-permute-start.24) | collective-permute-done | bytes 2080 | tf_op jit(solution)/shard_map/ppermute | solution.py:168
  208.3 3.3 %collective-permute-start.25 = (f32[4,64]{0,1:T(8,128)S(1)}, f32[4,64]{0,1:T(8,128)S(1)}, u32[]{:S(2)}, u32[]{:S(2)}) collective-permute-start(f32[4,64]{0,1:T(8,128)S(1)} %slice_select_fusion.7), channel_id=1, source_target_pairs={{0,4},{4,0},{8,12},{12,8},{1,5},{5,1},{9,13},{13,9},{2,6},{6,2},{1... | collective-permute-start | bytes 3080 | tf_op jit(solution)/shard_map/ppermute | solution.py:168
  215.1 2.2 %collective-permute-done.26 = f32[4,32]{0,1:T(8,128)S(1)} collective-permute-done((f32[4,32]{0,1:T(8,128)S(1)}, f32[4,32]{0,1:T(8,128)S(1)}, u32[]{:S(2)}, u32[]{:S(2)}) %collective-permute-start.26) | collective-permute-done | bytes 544 | tf_op jit(solution)/shard_map/ppermute | solution.py:168
  (115 shorter events, 49.6 us)
Async XLA Ops:
  0.0 36.5 %collective-permute-start.6 = (f32[24,3584]{1,0:T(8,128)}, f32[24,3584]{1,0:T(8,128)}, u32[]{:S(2)}, u32[]{:S(2)}) collective-permute-start(f32[24,3584]{1,0:T(8,128)} %param.10), channel_id=1, source_target_pairs={{0,4},{4,8},{8,12},{12,0},{1,5},{5,9},{9,13},{13,1},{2,6},{6,10},{... | collective-permute-start | bytes 1032200 | tf_op jit(solution)/shard_map/ppermute | solution.py:151
  3.0 49.1 %collective-permute-start.7 = (f32[24,3584]{1,0:T(8,128)}, f32[24,3584]{1,0:T(8,128)}, u32[]{:S(2)}, u32[]{:S(2)}) collective-permute-start(f32[24,3584]{1,0:T(8,128)} %param.10), channel_id=1, source_target_pairs={{0,8},{4,12},{8,0},{12,4},{1,9},{5,13},{9,1},{13,5},{2,10},{6,14},... | collective-permute-start | bytes 1032200 | tf_op jit(solution)/shard_map/ppermute | solution.py:151
  7.7 31.9 %collective-permute-start.12 = (f32[64,1024]{1,0:T(8,128)}, f32[64,1024]{1,0:T(8,128)}, u32[]{:S(2)}, u32[]{:S(2)}) collective-permute-start(f32[64,1024]{1,0:T(8,128)} %select_n.272), channel_id=1, source_target_pairs={{0,4},{4,8},{8,12},{12,0},{1,5},{5,9},{9,13},{13,1},{2,6},{6,10},{... | collective-permute-start | bytes 786440 | tf_op jit(solution)/shard_map/ppermute | solution.py:151
  7.7 37.5 %collective-permute-start.14 = (f32[64,1024]{1,0:T(8,128)}, f32[64,1024]{1,0:T(8,128)}, u32[]{:S(2)}, u32[]{:S(2)}) collective-permute-start(f32[64,1024]{1,0:T(8,128)} %select_n.272), channel_id=1, source_target_pairs={{0,8},{4,12},{8,0},{12,4},{1,9},{5,13},{9,1},{13,5},{2,10},{6,14},... | collective-permute-start | bytes 786440 | tf_op jit(solution)/shard_map/ppermute | solution.py:151
  9.6 11.7 %collective-permute-start = (f32[24,1024]{1,0:T(8,128)}, f32[24,1024]{1,0:T(8,128)}, u32[]{:S(2)}, u32[]{:S(2)}) collective-permute-start(f32[24,1024]{1,0:T(8,128)} %param.11), channel_id=1, source_target_pairs={{0,1},{1,0},{2,3},{3,2},{4,5},{5,4},{6,7},{7,6},{8,9},{9,8},{10,11... | collective-permute-start | bytes 294920 | tf_op jit(solution)/shard_map/ppermute | solution.py:136
  22.2 7.4 %collective-permute-start.1 = (f32[48,1024]{1,0:T(8,128)S(1)}, f32[48,1024]{1,0:T(8,128)S(1)}, u32[]{:S(2)}, u32[]{:S(2)}) collective-permute-start(f32[48,1024]{1,0:T(8,128)S(1)} %maximum_select_fusion.9), channel_id=1, source_target_pairs={{0,2},{2,0},{1,3},{3,1},{4,6},{6,4},{5,7},{7,5},{8,10},{10,8},{9,1... | collective-permute-start | bytes 589832 | tf_op jit(solution)/shard_map/ppermute | solution.py:136
  29.6 31.9 %collective-permute-start.18 = (f32[64,3584]{1,0:T(8,128)S(1)}, f32[64,3584]{1,0:T(8,128)S(1)}, u32[]{:S(2)}, u32[]{:S(2)}) collective-permute-start(f32[64,3584]{1,0:T(8,128)S(1)} %select_n.284), channel_id=1, source_target_pairs={{0,2},{2,0},{1,3},{3,1},{4,6},{6,4},{5,7},{7,5},{8,10},{10,8},{9,1... | collective-permute-start | bytes 2752520 | tf_op jit(solution)/shard_map/ppermute | solution.py:136
  36.5 14.1 %collective-permute-start.16 = (f32[64,1024]{1,0:T(8,128)}, f32[64,1024]{1,0:T(8,128)S(1)}, u32[]{:S(2)}, u32[]{:S(2)}) collective-permute-start(f32[64,1024]{1,0:T(8,128)} %select_n.272), channel_id=1, source_target_pairs={{0,12},{4,0},{8,4},{12,8},{1,13},{5,1},{9,5},{13,9},{2,14},{6,2},{... | collective-permute-start | bytes 786440 | tf_op jit(solution)/shard_map/ppermute | solution.py:151
  39.5 18.4 %collective-permute-start.8 = (f32[24,3584]{1,0:T(8,128)S(1)}, f32[24,3584]{1,0:T(8,128)S(1)}, u32[]{:S(2)}, u32[]{:S(2)}) collective-permute-start(f32[24,3584]{1,0:T(8,128)S(1)} %copy-done.7), channel_id=1, source_target_pairs={{0,12},{4,0},{8,4},{12,8},{1,13},{5,1},{9,5},{13,9},{2,14},{6,2},{... | collective-permute-start | bytes 1032200 | tf_op jit(solution)/shard_map/ppermute | solution.py:151
  45.2 46.9 %collective-permute-start.13 = (f32[64,1024]{1,0:T(8,128)}, f32[64,1024]{1,0:T(8,128)S(1)}, u32[]{:S(2)}, u32[]{:S(2)}) collective-permute-start(f32[64,1024]{1,0:T(8,128)} %collective-permute-done.12), channel_id=1, source_target_pairs={{0,16},{16,0},{1,17},{17,1},{2,18},{18,2},{3,19},{19,3},{4,20},{20... | collective-permute-start | bytes 786440 | tf_op jit(solution)/shard_map/ppermute | solution.py:136
  50.6 66.9 %collective-permute-start.15 = (f32[64,1024]{1,0:T(8,128)}, f32[64,1024]{1,0:T(8,128)S(1)}, u32[]{:S(2)}, u32[]{:S(2)}) collective-permute-start(f32[64,1024]{1,0:T(8,128)} %collective-permute-done.14), channel_id=1, source_target_pairs={{0,16},{16,0},{1,17},{17,1},{2,18},{18,2},{3,19},{19,3},{4,20},{20... | collective-permute-start | bytes 786440 | tf_op jit(solution)/shard_map/ppermute | solution.py:136
  52.2 66.6 %collective-permute-start.17 = (f32[64,1024]{1,0:T(8,128)S(1)}, f32[64,1024]{1,0:T(8,128)S(1)}, u32[]{:S(2)}, u32[]{:S(2)}) collective-permute-start(f32[64,1024]{1,0:T(8,128)S(1)} %collective-permute-done.16), channel_id=1, source_target_pairs={{0,16},{16,0},{1,17},{17,1},{2,18},{18,2},{3,19},{19,3},{4,20},{20... | collective-permute-start | bytes 786440 | tf_op jit(solution)/shard_map/ppermute | solution.py:136
  57.9 34.0 %collective-permute-start.2 = (f32[48,1024]{1,0:T(8,128)S(1)}, f32[48,1024]{1,0:T(8,128)S(1)}, u32[]{:S(2)}, u32[]{:S(2)}) collective-permute-start(f32[48,1024]{1,0:T(8,128)S(1)} %slice_select_fusion.4), channel_id=1, source_target_pairs={{0,4},{4,0},{8,12},{12,8},{1,5},{5,1},{9,13},{13,9},{2,6},{6,2},{1... | collective-permute-start | bytes 589832 | tf_op jit(solution)/shard_map/ppermute | solution.py:168
  61.5 27.6 %collective-permute-start.19 = (f32[64,3584]{1,0:T(8,128)S(1)}, f32[64,3584]{1,0:T(8,128)S(1)}, u32[]{:S(2)}, u32[]{:S(2)}) collective-permute-start(f32[64,3584]{1,0:T(8,128)S(1)} %collective-permute-done.18), channel_id=1, source_target_pairs={{0,16},{16,0},{1,17},{17,1},{2,18},{18,2},{3,19},{19,3},{4,20},{20... | collective-permute-start | bytes 2752520 | tf_op jit(solution)/shard_map/ppermute | solution.py:136
  90.9 32.9 %collective-permute-start.20 = (f32[256,3584]{1,0:T(8,128)S(1)}, f32[256,3584]{1,0:T(8,128)S(1)}, u32[]{:S(2)}, u32[]{:S(2)}) collective-permute-start(f32[256,3584]{1,0:T(8,128)S(1)} %maximum_select_fusion), channel_id=1, source_target_pairs={{0,1},{1,0},{2,3},{3,2},{4,5},{5,4},{6,7},{7,6},{8,9},{9,8},{10,11... | collective-permute-start | bytes 11010056 | tf_op jit(solution)/shard_map/ppermute | solution.py:136
  91.9 7.1 %collective-permute-start.21 = (f32[48,1792]{1,0:T(8,128)S(1)}, f32[48,1792]{1,0:T(8,128)S(1)}, u32[]{:S(2)}, u32[]{:S(2)}) collective-permute-start(f32[48,1792]{1,0:T(8,128)S(1)} %slice_select_fusion.1), channel_id=1, source_target_pairs={{0,1},{1,0},{2,3},{3,2},{4,5},{5,4},{6,7},{7,6},{8,9},{9,8},{10,11... | collective-permute-start | bytes 1032200 | tf_op jit(solution)/shard_map/ppermute | solution.py:136
  92.1 6.8 %collective-permute-start.3 = (f32[24,1024]{1,0:T(8,128)S(1)}, f32[24,1024]{1,0:T(8,128)S(1)}, u32[]{:S(2)}, u32[]{:S(2)}) collective-permute-start(f32[24,1024]{1,0:T(8,128)S(1)} %slice_select_fusion.5), channel_id=1, source_target_pairs={{0,8},{4,12},{8,0},{12,4},{1,9},{5,13},{9,1},{13,5},{2,10},{6,14},... | collective-permute-start | bytes 294920 | tf_op jit(solution)/shard_map/ppermute | solution.py:168
  99.0 6.3 %collective-permute-start.4 = (f32[24,1024]{1,0:T(8,128)S(1)}, f32[24,1024]{1,0:T(8,128)S(1)}, u32[]{:S(2)}, u32[]{:S(2)}) collective-permute-start(f32[24,1024]{1,0:T(8,128)S(1)} %select_add_fusion.3), channel_id=1, source_target_pairs={{0,8},{4,12},{8,0},{12,4},{1,9},{5,13},{9,1},{13,5},{2,10},{6,14},... | collective-permute-start | bytes 294920 | tf_op jit(solution)/shard_map/ppermute | solution.py:168
  101.8 11.0 %collective-permute-start.22 = (f32[48,1792]{1,0:T(8,128)S(1)}, f32[48,1792]{1,0:T(8,128)S(1)}, u32[]{:S(2)}, u32[]{:S(2)}) collective-permute-start(f32[48,1792]{1,0:T(8,128)S(1)} %select_add_fusion), channel_id=1, source_target_pairs={{0,2},{2,0},{1,3},{3,1},{4,6},{6,4},{5,7},{7,5},{8,10},{10,8},{9,1... | collective-permute-start | bytes 1032200 | tf_op jit(solution)/shard_map/ppermute | solution.py:136
  105.2 14.1 %collective-permute-start.10 = (f32[48,1792]{1,0:T(8,128)S(1)}, f32[48,1792]{1,0:T(8,128)S(1)}, u32[]{:S(2)}, u32[]{:S(2)}) collective-permute-start(f32[48,1792]{1,0:T(8,128)S(1)} %select_add_fusion.1), channel_id=1, source_target_pairs={{0,2},{2,0},{1,3},{3,1},{4,6},{6,4},{5,7},{7,5},{8,10},{10,8},{9,1... | collective-permute-start | bytes 1032200 | tf_op jit(solution)/shard_map/ppermute | solution.py:136
  112.7 8.5 %collective-permute-start.5 = (f32[48,1024]{1,0:T(8,128)S(1)}, f32[48,1024]{1,0:T(8,128)S(1)}, u32[]{:S(2)}, u32[]{:S(2)}) collective-permute-start(f32[48,1024]{1,0:T(8,128)S(1)} %maximum_select_fusion.10), channel_id=1, source_target_pairs={{0,4},{4,0},{8,12},{12,8},{1,5},{5,1},{9,13},{13,9},{2,6},{6,2},{1... | collective-permute-start | bytes 589832 | tf_op jit(solution)/shard_map/ppermute | solution.py:168
  117.5 4.5 %collective-permute-start.23 = (f32[48,1792]{1,0:T(8,128)S(1)}, f32[48,1792]{1,0:T(8,128)S(1)}, u32[]{:S(2)}, u32[]{:S(2)}) collective-permute-start(f32[48,1792]{1,0:T(8,128)S(1)} %add.95), channel_id=1, source_target_pairs={{0,1},{1,0},{2,3},{3,2},{4,5},{5,4},{6,7},{7,6},{8,9},{9,8},{10,11... | collective-permute-start | bytes 1032200 | tf_op jit(solution)/shard_map/ppermute | solution.py:136
  203.0 5.2 %collective-permute-start.24 = (f32[4,128]{0,1:T(8,128)S(1)}, f32[4,128]{0,1:T(8,128)S(1)}, u32[]{:S(2)}, u32[]{:S(2)}) collective-permute-start(f32[4,128]{0,1:T(8,128)S(1)} %slice_select_fusion.6), channel_id=1, source_target_pairs={{0,8},{4,12},{8,0},{12,4},{1,9},{5,13},{9,1},{13,5},{2,10},{6,14},... | collective-permute-start | bytes 6152 | tf_op jit(solution)/shard_map/ppermute | solution.py:168
  208.3 5.2 %collective-permute-start.25 = (f32[4,64]{0,1:T(8,128)S(1)}, f32[4,64]{0,1:T(8,128)S(1)}, u32[]{:S(2)}, u32[]{:S(2)}) collective-permute-start(f32[4,64]{0,1:T(8,128)S(1)} %slice_select_fusion.7), channel_id=1, source_target_pairs={{0,4},{4,0},{8,12},{12,8},{1,5},{5,1},{9,13},{13,9},{2,6},{6,2},{1... | collective-permute-start | bytes 3080 | tf_op jit(solution)/shard_map/ppermute | solution.py:168
  (16 other events, 83.5 us)

commit v2 on v1

--- a/solution.py
+++ b/solution.py
@@ -66,19 +66,26 @@
     )(x, basis)
 
 
-def score_kernel(ids_ref, damping_ref, acts_ref, grads_ref, eig_ref, right_ref, left_ref, out_ref, weighted, right_high, right_low):
+def score_kernel(ids_ref, damping_ref, acts_ref, grads_ref, eig_ref, right_ref, left_ref, left_ref_2, out_ref, chosen, weighted, right_high, right_low):
     tokens, inner = acts_ref.shape
+    span = tokens // 2
 
     @pl.when(pl.program_id(0) == 0)
     def _():
         out_ref[...] = jnp.zeros_like(out_ref)
+        ids = ids_ref[...]
+        acts_high, acts_low = halves(acts_ref[...])
+        place_in = lax.broadcasted_iota(jnp.int32, (span, tokens), 0)
+        token = lax.broadcasted_iota(jnp.int32, (span, tokens), 1)
         for s in range(SEQS):
-            member = ids_ref[...] == s
-            high, low = halves(jnp.where(member, acts_ref[...], 0.0))
+            start = jnp.sum((ids < s).astype(jnp.int32), axis=1, keepdims=True)
+            pick = jnp.where((ids == s) & (token - start == place_in), 1.0, 0.0).astype(BF16)
+            chosen[s * span : (s + 1) * span, :] = pick
+            high = dot(pick, acts_high).astype(BF16)
             cols = slice(s * inner, (s + 1) * inner)
-            weighted[:tokens, cols] = high
-            weighted[tokens : 2 * tokens, cols] = low
-            weighted[2 * tokens :, cols] = high
+            weighted[:span, cols] = high
+            weighted[span : 2 * span, cols] = dot(pick, acts_low).astype(BF16)
+            weighted[2 * span :, cols] = high
         high, low = halves(right_ref[...].T)
         right_high[...] = high
         right_low[...] = low
@@ -86,9 +93,12 @@
     rows = eig_ref.shape[0]
     inverse = 1.0 / (eig_ref[...] + damping_ref[0])
     grad_high, grad_low = halves(grads_ref[...])
-    grad_all = jnp.concatenate([grad_high, grad_high, grad_low], axis=0)
-    left = left_ref[...].T
+    grad_high = dot(chosen[...], grad_high).astype(BF16)
+    grad_low = dot(chosen[...], grad_low).astype(BF16)
+    left = jnp.concatenate([left_ref[...].T, left_ref_2[...].T], axis=1)
     for s in range(SEQS):
+        own = slice(s * span, (s + 1) * span)
+        grad_all = jnp.concatenate([grad_high[own], grad_high[own], grad_low[own]], axis=0)
         grad_seq = dot(grad_all, weighted[:, s * inner : (s + 1) * inner], ((0,), (0,)))
         high, low = halves(grad_seq * inverse)
         cross = dot(high, right_high[...]) + dot(high, right_low[...]) + dot(low, right_high[...])
@@ -96,29 +106,31 @@
         out_ref[s * 8 : (s + 1) * 8, :] += jnp.sum(terms, axis=0)
 
 
-def score(ids, damping, acts, grads, eigenvalues, right, left, part, parts):
+def score(ids, damping, acts, grads, eigenvalues, right, lefts):
     tokens, inner = acts.shape
     queries = right.shape[0]
-    outer = eigenvalues.shape[0] // parts
-    tile = tile_of(outer, 256)
+    outer = eigenvalues.shape[0]
+    tile = tile_of(outer, 512)
     steps = outer // tile
     whole = lambda i: (0, 0)
     return pl.pallas_call(
         score_kernel,
         grid=(steps,),
         in_specs=[
-            pl.BlockSpec((tokens, 1), whole),
+            pl.BlockSpec((1, tokens), whole),
             pl.BlockSpec(memory_space=pltpu.SMEM),
             pl.BlockSpec((tokens, inner), whole),
             pl.BlockSpec((tokens, tile), lambda i: (0, i)),
-            pl.BlockSpec((tile, inner), lambda i: (part * steps + i, 0)),
+            pl.BlockSpec((tile, inner), lambda i: (i, 0)),
             pl.BlockSpec((queries, inner), whole),
-            pl.BlockSpec((queries, tile), lambda i: (0, part * steps + i)),
+            pl.BlockSpec((queries // 2, tile), lambda i: (0, i)),
+            pl.BlockSpec((queries // 2, tile), lambda i: (0, i)),
         ],
         out_specs=pl.BlockSpec((SEQS * 8, queries), whole),
         out_shape=jax.ShapeDtypeStruct((SEQS * 8, queries), F32),
         scratch_shapes=[
-            pltpu.VMEM((3 * tokens, SEQS * inner), BF16),
+            pltpu.VMEM((SEQS * (tokens // 2), tokens), BF16),
+            pltpu.VMEM((3 * (tokens // 2), SEQS * inner), BF16),
             pltpu.VMEM((inner, queries), BF16),
             pltpu.VMEM((inner, queries), BF16),
         ],
@@ -129,7 +141,7 @@
             transcendentals=0,
         ),
         name="score",
-    )(ids.reshape(tokens, 1), damping, acts, grads, eigenvalues, right, left)
+    )(ids.reshape(1, tokens), damping, acts, grads, eigenvalues, right, *lefts)
 
 
 def swap(x, axis):
@@ -209,50 +221,64 @@
 ):
     groups, factor, dp, core = sizes
     small = groups == 2 and factor == 4 and dp == 2 and core == 2
-    parts = 2 if small else 1
     flat_out = query_out.reshape(-1, query_out.shape[2])
     flat_in = query_in.reshape(-1, query_in.shape[2])
     if small:
         g = lax.axis_index("groups")
         x = lax.axis_index("dp")
         c = lax.axis_index("query")
+        tie = lax.optimization_barrier
         pair = join(act_factors, swap(act_factors, "query"), c)
         acts_all = join(pair, swap(pair, "dp"), x)
         grads_all = place(*gather_line(grad_factors, "factor", factor), factor)
-        half_in, at = gather_line(my_half(flat_in, g, True), "factor", factor)
-        blocks = [flat_in] + [join(b, swap(b, "groups"), g) for b in half_in[1:]]
+        half_out = swap(my_half(flat_out, g, True), "dp")
+        acts_all, grads_all, flat_in, half_out = tie((acts_all, grads_all, flat_in, half_out))
+        act_part = rotate(acts_all, in_basis, 0, 1)
+        half_in, _ = gather_line(my_half(flat_in, g, True), "factor", factor)
+        half_out_2 = swap(half_out, "groups")
+        act_part, grads_all = tie((act_part, grads_all))
+        first = rotate(grads_all, out_basis, 0, 2)
+        first, grads_all, half_out_2, half_in = tie((first, grads_all, half_out_2, half_in))
+        sent = jnp.concatenate(half_in[1:])
+        got = swap(sent, "groups")
+        own_core = join(flat_out, join(half_out, half_out_2, g), x)
+        other_core = swap(own_core, "query")
+        second = rotate(grads_all, out_basis, 1, 2)
+        second, got, other_core = tie((second, got, other_core))
+        rot_act = sum_line(act_part, "factor", factor)
+        rot_grad = jnp.concatenate([first, second], axis=1)
+        mine = my_half(rot_grad, c, True) + swap(my_half(rot_grad, c, False), "query")
+        mine = mine + swap(mine, "dp")
+        rot_grad = join(mine, swap(mine, "query"), c)
+        rows = half_in[0].shape[0]
+        pieces = [(sent[k * rows : (k + 1) * rows], got[k * rows : (k + 1) * rows]) for k in range(factor - 1)]
+        blocks = [flat_in] + [join(b, o, g) for b, o in pieces]
+        me = lax.axis_index("factor")
+        at = []
+        for shift in range(factor):
+            owner = lax.rem(me + factor - shift, factor)
+            at.append(jnp.where(lax.rem(owner, 2) == c, owner // 2, 2 + owner // 2))
         right = place(blocks, at, factor)
-        half_out = swap(my_half(flat_out, g, True), "dp")
-        other_chip = join(half_out, swap(half_out, "groups"), g)
-        own_core = join(flat_out, other_chip, x)
-        other_core = swap(own_core, "query")
-        rows = flat_out.shape[0]
-        low = jnp.where(c == 0, own_core, other_core)
-        high = jnp.where(c == 0, other_core, own_core)
-        left = jnp.concatenate([low[:rows], high[:rows], low[rows:], high[rows:]])
+        lefts = (own_core, other_core)
     else:
         acts_all = lax.all_gather(act_factors, ("dp", "query"), axis=0, tiled=True)
         grads_all = lax.all_gather(grad_factors, "factor", axis=0, tiled=True)
         right = lax.all_gather(flat_in, "factor", axis=0, tiled=True)
         left = lax.all_gather(flat_out, ("dp", "query"), axis=0, tiled=True)
-
-    rot_act = rotate(acts_all, in_basis, 0, 1)
-    rot_act = sum_line(rot_act, "factor", factor) if small else lax.psum(rot_act, "factor")
-
-    total = None
-    for part in range(parts):
-        rot_grad = rotate(grads_all, out_basis, part, parts)
-        if small:
-            mine = my_half(rot_grad, c, True) + swap(my_half(rot_grad, c, False), "query")
-            mine = mine + swap(mine, "dp")
-            rot_grad = join(mine, swap(mine, "query"), c)
-        else:
-            rot_grad = lax.psum(rot_grad, ("dp", "query"))
-        one = score(seq_ids, damping, rot_act, rot_grad, eigenvalues, right, left, part, parts)
-        total = one if total is None else total + one
-
+        lefts = (left[: left.shape[0] // 2], left[left.shape[0] // 2 :])
+        rot_act = lax.psum(rotate(acts_all, in_basis, 0, 1), "factor")
+        rot_grad = lax.psum(rotate(grads_all, out_basis, 0, 1), ("dp", "query"))
+
+    total = score(seq_ids, damping, rot_act, rot_grad, eigenvalues, right, lefts)
     count = query_ids.shape[0]
     raw = jnp.sum(total.reshape(SEQS, 8, count, -1), axis=(1, 3))
+    if small:
+        b = jnp.split(raw, 4, axis=1)
+        raw = jnp.where(
+            c == 0,
+            jnp.concatenate([b[0], b[2], b[1], b[3]], axis=1),
+            jnp.concatenate([b[2], b[0], b[3], b[1]], axis=1),
+        )
     raw = raw[:, query_ids]
     return scatter_sum(raw, ("factor", "dp", "query"), (factor, dp, core))
 

time: 220 us -> 212 us (0.964)
  waiting for transfers between devices: 39.9 us -> 69.8 us
  starting transfers between devices: 41.7 us -> 19.5 us
  Pallas kernels: 102 us -> 90.7 us
  other arithmetic: 19.1 us -> 14.9 us
    ppermute x14 -> x9, waiting for transfers between devices: 12 us -> 33.7 us  [swap(): return lax.ppermute(x, axis, [(0, 1), (1, 0)])]
    ppermute x8, starting transfers between devices: 20.8 us -> 3.46 us  [flip(): return lax.ppermute(x, axis, [(i, i ^ bit) for i in range(size)])]
    ppermute x8, waiting for transfers between devices: 15.1 us -> 31.2 us  [flip(): return lax.ppermute(x, axis, [(i, i ^ bit) for i in range(size)])]
    pallas_call x2 -> x1, Pallas kernels: 72.2 us -> 61.2 us  [score(): pl.pallas_call(score_kernel, grid=(steps,), in_specs=[pl.BlockSpec((1, to...]
    ppermute x6, waiting for transfers between devices: 12.8 us -> 4.8 us  [gather_line(): lax.ppermute(x, axis, [(i, (i + shift) % size) for i in range(size)])]
    ppermute x14 -> x9, starting transfers between devices: 10.4 us -> 5.82 us  [swap(): return lax.ppermute(x, axis, [(0, 1), (1, 0)])]
    select_n x8 -> x7, other arithmetic: 4.92 us -> 8.38 us  [join(): jnp.where(index == 0, jnp.concatenate([mine, other]), jnp.concatenate([ot...]
    unnamed x24 -> x21, local copies, waits for them, and re-layouts: 3.32 us -> 0.57 us
  transfers between devices with their start and end apart: 28 -> 23, of which waited for: 13 -> 12; matrix products, arithmetic and copies ran while one was open for 11% -> 9% of each run, Pallas kernels for 13% -> 14%
where the time goes in v2:
time: 212 us
  Pallas kernels  90.7 us (43%)
  waiting for transfers between devices  69.8 us (33%)
  starting transfers between devices  19.5 us (9%)
  local copies, waits for them, and re-layouts  15.6 us (7%)
  other arithmetic  14.9 us (7%)
    pallas_call x1, Pallas kernels, score(): pl.pallas_call(score_kernel, grid=(steps,), in_specs=[pl.BlockSpec((1, to...  61.2 us
    ppermute x9, waiting for transfers between devices, swap(): return lax.ppermute(x, axis, [(0, 1), (1, 0)])  33.7 us
    ppermute x8, waiting for transfers between devices, flip(): return lax.ppermute(x, axis, [(i, i ^ bit) for i in range(size)])  31.2 us
    pallas_call x3, Pallas kernels, rotate(): pl.pallas_call(rotate_kernel, grid=(steps,), in_specs=[pl.BlockSpec((rows...  29.6 us
    ppermute x6, starting transfers between devices, gather_line(): lax.ppermute(x, axis, [(i, (i + shift) % size) for i in range(size)])  10.3 us
    select_n x7, other arithmetic, join(): jnp.where(index == 0, jnp.concatenate([mine, other]), jnp.concatenate([ot...  8.38 us
    ppermute x9, starting transfers between devices, swap(): return lax.ppermute(x, axis, [(0, 1), (1, 0)])  5.82 us
    ppermute x6, waiting for transfers between devices, gather_line(): lax.ppermute(x, axis, [(i, (i + shift) % size) for i in range(size)])  4.8 us
  transfers between devices with their start and end apart: 23, of which 12 were waited for; matrix products, arithmetic and copies ran while one was open for 9% of the time, Pallas kernels for 14%

profile of v2, /device:TPU:0, one launch (start us, length us, event | category | flops | bytes accessed | tf_op | source)
XLA Modules:
  0.0 211.7 jit_solution(12930457481570110759)
XLA Ops:
  0.0 3.0 %collective-permute-start.2 = (f32[24,3584]{1,0:T(8,128)}, f32[24,3584]{1,0:T(8,128)}, u32[]{:S(2)}, u32[]{:S(2)}) collective-permute-start(f32[24,3584]{1,0:T(8,128)} %param.10), channel_id=1, source_target_pairs={{0,4},{4,8},{8,12},{12,0},{1,5},{5,9},{9,13},{13,1},{2,6},{6,10},{... | collective-permute-start | bytes 1032200 | tf_op jit(solution)/shard_map/ppermute | solution.py:163
  3.0 2.0 collective-permute-start.4
  6.1 2.0 slice_select_fusion
  11.9 2.3 %reshape.17 = f32[128,1024]{1,0:T(8,128)} reshape(f32[64,2,1024]{2,1,0:T(2,128)} %param.18) | data formatting | bytes 1048576 | tf_op jit(solution)/shard_map/reshape | solution.py:225
  14.3 22.6 %collective-permute-done.1 = f32[48,1024]{1,0:T(8,128)} collective-permute-done((f32[48,1024]{1,0:T(8,128)S(1)}, f32[48,1024]{1,0:T(8,128)}, u32[]{:S(2)}, u32[]{:S(2)}) %collective-permute-start.1) | collective-permute-done | bytes 196640 | tf_op jit(solution)/shard_map/ppermute | solution.py:148
  36.9 1.8 maximum_select_fusion.6.x_ref
  41.8 1.6 collective-permute-start.10
  43.4 2.5 %reshape.18 = f32[128,3584]{1,0:T(8,128)} reshape(f32[64,2,3584]{2,1,0:T(2,128)S(1)} %copy-done.1) | data formatting | bytes 3670016 | tf_op jit(solution)/shard_map/reshape | solution.py:224
  48.4 1.7 collective-permute-start.12
  51.2 3.6 %rotate.3 = f32[96,1024]{1,0:T(8,128)} custom-call(f32[96,1024]{1,0:T(8,128)} %maximum_select_fusion.6.x_ref, f32[1024,1024]{1,0:T(8,128)} %basis_ref.3), custom_call_target="tpu_custom_call" | custom-call | flops 603979776 | bytes 4194304 | tf_op jit(solution)/shard_map/rotate/pallas_call | solution.py:51
  54.8 13.0 %rotate.4 = f32[96,1792]{1,0:T(8,128)} custom-call(f32[96,3584]{1,0:T(8,128)} %copy-done, f32[3584,3584]{1,0:T(8,128)} %basis_ref.5), custom_call_target="tpu_custom_call" | custom-call | flops 3699376128 | bytes 25690112 | tf_op jit(solution)/shard_map/rotate/pallas_call | solution.py:51
  67.8 4.8 %collective-permute-done.12 = f32[64,1024]{1,0:T(8,128)S(1)} collective-permute-done((f32[64,1024]{1,0:T(8,128)S(1)}, f32[64,1024]{1,0:T(8,128)S(1)}, u32[]{:S(2)}, u32[]{:S(2)}) %collective-permute-start.12) | collective-permute-done | bytes 262176 | tf_op jit(solution)/shard_map/ppermute | solution.py:163
  72.6 2.2 %maximum_select_fusion.1 = f32[128,3584]{1,0:T(8,128)S(1)} fusion(f32[64,3584]{1,0:T(8,128)} %collective-permute-done.10, f32[64,3584]{1,0:T(8,128)} %collective-permute-done.5, pred[]{:T(512)S(6)} %eq.67), kind=kLoop, calls=%fused_computation.2 | loop fusion | flops 1376256 | bytes 3670017 | tf_op jit(solution)/shard_map/jit(_where)/select_n | solution.py:176
  74.8 2.1 %maximum_select_fusion.left_ref = f32[256,3584]{1,0:T(8,128)} fusion(f32[128,3584]{1,0:T(8,128)S(1)} %maximum_select_fusion.1, f32[128,3584]{1,0:T(8,128)S(1)} %copy-done.2, pred[]{:T(512)S(6)} %eq.64), kind=kLoop, calls=%fused_computation.1 | loop fusion | flops 2752512 | bytes 7340033 | tf_op jit(solution)/shard_map/jit(_where)/select_n | solution.py:176
  78.5 13.0 %rotate.5 = f32[96,1792]{1,0:T(8,128)} custom-call(f32[96,3584]{1,0:T(8,128)} %copy-done, f32[3584,3584]{1,0:T(8,128)} %basis_ref.5), custom_call_target="tpu_custom_call" | custom-call | flops 3699376128 | bytes 25690112 | tf_op jit(solution)/shard_map/rotate/pallas_call | solution.py:51
  91.5 6.7 %collective-permute-done.14 = f32[192,1024]{1,0:T(8,128)} collective-permute-done((f32[192,1024]{1,0:T(8,128)}, f32[192,1024]{1,0:T(8,128)}, u32[]{:S(2)}, u32[]{:S(2)}) %collective-permute-start.14) | collective-permute-done | bytes 786464 | tf_op jit(solution)/shard_map/ppermute | solution.py:148
  101.1 7.5 %collective-permute-done.6 = f32[48,1024]{1,0:T(8,128)S(1)} collective-permute-done((f32[48,1024]{1,0:T(8,128)}, f32[48,1024]{1,0:T(8,128)S(1)}, u32[]{:S(2)}, u32[]{:S(2)}) %collective-permute-start.6) | collective-permute-done | bytes 196640 | tf_op jit(solution)/shard_map/ppermute | solution.py:180
  111.7 4.4 %collective-permute-done.7 = f32[24,1024]{1,0:T(8,128)S(1)} collective-permute-done((f32[24,1024]{1,0:T(8,128)S(1)}, f32[24,1024]{1,0:T(8,128)S(1)}, u32[]{:S(2)}, u32[]{:S(2)}) %collective-permute-start.7) | collective-permute-done | bytes 98336 | tf_op jit(solution)/shard_map/ppermute | solution.py:180
  117.0 5.2 %collective-permute-done.8 = f32[24,1024]{1,0:T(8,128)S(1)} collective-permute-done((f32[24,1024]{1,0:T(8,128)S(1)}, f32[24,1024]{1,0:T(8,128)S(1)}, u32[]{:S(2)}, u32[]{:S(2)}) %collective-permute-start.8) | collective-permute-done | bytes 98336 | tf_op jit(solution)/shard_map/ppermute | solution.py:180
  122.6 4.4 %collective-permute-done.17 = f32[48,3584]{1,0:T(8,128)S(1)} collective-permute-done((f32[48,3584]{1,0:T(8,128)S(1)}, f32[48,3584]{1,0:T(8,128)S(1)}, u32[]{:S(2)}, u32[]{:S(2)}) %collective-permute-start.17) | collective-permute-done | bytes 688160 | tf_op jit(solution)/shard_map/ppermute | solution.py:148
  132.6 61.2 %score.1 = f32[32,512]{1,0:T(8,128)} custom-call(s32[1,96]{1,0:T(1,128)} %bitcast.6, f32[1]{0:T(128)S(6)} %copy.41.damping_ref, f32[96,1024]{1,0:T(8,128)} %maximum_select_fusion.7.acts_ref, f32[96,3584]{1,0:T(8,128)} %maximum_select_fusion.2.grads_ref, f32[3584,1024]{1,0:T(8,128)} %eig_ref.1, f32[512,1024]{1,0:T(8,128)} %copy-done.6, ...), custom_call_target="tpu_custom_call" | custom-call | flops 62008590336 | bytes 22020096 | tf_op jit(solution)/shard_map/score/pallas_call | solution.py:116
  196.6 5.4 %collective-permute-done.19 = f32[4,128]{0,1:T(8,128)S(1)} collective-permute-done((f32[4,128]{0,1:T(8,128)S(1)}, f32[4,128]{0,1:T(8,128)S(1)}, u32[]{:S(2)}, u32[]{:S(2)}) %collective-permute-start.19) | collective-permute-done | bytes 2080 | tf_op jit(solution)/shard_map/ppermute | solution.py:180
  202.1 3.9 %collective-permute-done.20 = f32[4,64]{0,1:T(8,128)S(1)} collective-permute-done((f32[4,64]{0,1:T(8,128)S(1)}, f32[4,64]{0,1:T(8,128)S(1)}, u32[]{:S(2)}, u32[]{:S(2)}) %collective-permute-start.20) | collective-permute-done | bytes 1056 | tf_op jit(solution)/shard_map/ppermute | solution.py:180
  207.5 2.2 %collective-permute-done.21 = f32[4,32]{0,1:T(8,128)S(1)} collective-permute-done((f32[4,32]{0,1:T(8,128)S(1)}, f32[4,32]{0,1:T(8,128)S(1)}, u32[]{:S(2)}, u32[]{:S(2)}) %collective-permute-start.21) | collective-permute-done | bytes 544 | tf_op jit(solution)/shard_map/ppermute | solution.py:180
  (96 shorter events, 31.3 us)
Async XLA Ops:
  0.0 38.8 %collective-permute-start.2 = (f32[24,3584]{1,0:T(8,128)}, f32[24,3584]{1,0:T(8,128)}, u32[]{:S(2)}, u32[]{:S(2)}) collective-permute-start(f32[24,3584]{1,0:T(8,128)} %param.10), channel_id=1, source_target_pairs={{0,4},{4,8},{8,12},{12,0},{1,5},{5,9},{9,13},{13,1},{2,6},{6,10},{... | collective-permute-start | bytes 1032200 | tf_op jit(solution)/shard_map/ppermute | solution.py:163
  3.0 37.8 %collective-permute-start.4 = (f32[24,3584]{1,0:T(8,128)}, f32[24,3584]{1,0:T(8,128)}, u32[]{:S(2)}, u32[]{:S(2)}) collective-permute-start(f32[24,3584]{1,0:T(8,128)} %param.10), channel_id=1, source_target_pairs={{0,12},{4,0},{8,4},{12,8},{1,13},{5,1},{9,5},{13,9},{2,14},{6,2},{... | collective-permute-start | bytes 1032200 | tf_op jit(solution)/shard_map/ppermute | solution.py:163
  5.1 34.7 %collective-permute-start.3 = (f32[24,3584]{1,0:T(8,128)}, f32[24,3584]{1,0:T(8,128)}, u32[]{:S(2)}, u32[]{:S(2)}) collective-permute-start(f32[24,3584]{1,0:T(8,128)} %param.10), channel_id=1, source_target_pairs={{0,8},{4,12},{8,0},{12,4},{1,9},{5,13},{9,1},{13,5},{2,10},{6,14},... | collective-permute-start | bytes 1032200 | tf_op jit(solution)/shard_map/ppermute | solution.py:163
  6.1 5.0 %collective-permute-start = (f32[24,1024]{1,0:T(8,128)}, f32[24,1024]{1,0:T(8,128)S(1)}, u32[]{:S(2)}, u32[]{:S(2)}) collective-permute-start(f32[24,1024]{1,0:T(8,128)} %param.11), channel_id=1, source_target_pairs={{0,1},{1,0},{2,3},{3,2},{4,5},{5,4},{6,7},{7,6},{8,9},{9,8},{10,11... | collective-permute-start | bytes 294920 | tf_op jit(solution)/shard_map/ppermute | solution.py:148
  9.6 32.2 %collective-permute-start.5 = (f32[64,3584]{1,0:T(8,128)}, f32[64,3584]{1,0:T(8,128)}, u32[]{:S(2)}, u32[]{:S(2)}) collective-permute-start(f32[64,3584]{1,0:T(8,128)} %select_n.268), channel_id=1, source_target_pairs={{0,2},{2,0},{1,3},{3,1},{4,6},{6,4},{5,7},{7,5},{8,10},{10,8},{9,1... | collective-permute-start | bytes 2752520 | tf_op jit(solution)/shard_map/ppermute | solution.py:148
  11.1 25.8 %collective-permute-start.1 = (f32[48,1024]{1,0:T(8,128)S(1)}, f32[48,1024]{1,0:T(8,128)}, u32[]{:S(2)}, u32[]{:S(2)}) collective-permute-start(f32[48,1024]{1,0:T(8,128)S(1)} %maximum_select_fusion.8), channel_id=1, source_target_pairs={{0,2},{2,0},{1,3},{3,1},{4,6},{6,4},{5,7},{7,5},{8,10},{10,8},{9,1... | collective-permute-start | bytes 589832 | tf_op jit(solution)/shard_map/ppermute | solution.py:148
  11.9 31.5 %copy-start.1 = (f32[64,2,3584]{2,1,0:T(2,128)S(1)}, f32[64,2,3584]{2,1,0:T(2,128)}, u32[]{:S(2)}) copy-start(f32[64,2,3584]{2,1,0:T(2,128)} %param.17) | copy-start | bytes 5505028
  41.8 30.7 %collective-permute-start.10 = (f32[64,3584]{1,0:T(8,128)}, f32[64,3584]{1,0:T(8,128)}, u32[]{:S(2)}, u32[]{:S(2)}) collective-permute-start(f32[64,3584]{1,0:T(8,128)} %collective-permute-done.5), channel_id=1, source_target_pairs={{0,16},{16,0},{1,17},{17,1},{2,18},{18,2},{3,19},{19,3},{4,20},{20... | collective-permute-start | bytes 2752520 | tf_op jit(solution)/shard_map/ppermute | solution.py:148
  47.0 20.8 %collective-permute-start.13 = (f32[64,1024]{1,0:T(8,128)S(1)}, f32[64,1024]{1,0:T(8,128)S(1)}, u32[]{:S(2)}, u32[]{:S(2)}) collective-permute-start(f32[64,1024]{1,0:T(8,128)S(1)} %slice_select_fusion.2), channel_id=1, source_target_pairs={{0,12},{4,0},{8,4},{12,8},{1,13},{5,1},{9,5},{13,9},{2,14},{6,2},{... | collective-permute-start | bytes 786440 | tf_op jit(solution)/shard_map/ppermute | solution.py:163
  48.4 24.2 %collective-permute-start.12 = (f32[64,1024]{1,0:T(8,128)S(1)}, f32[64,1024]{1,0:T(8,128)S(1)}, u32[]{:S(2)}, u32[]{:S(2)}) collective-permute-start(f32[64,1024]{1,0:T(8,128)S(1)} %slice_select_fusion.2), channel_id=1, source_target_pairs={{0,8},{4,12},{8,0},{12,4},{1,9},{5,13},{9,1},{13,5},{2,10},{6,14},... | collective-permute-start | bytes 786440 | tf_op jit(solution)/shard_map/ppermute | solution.py:163
  50.1 22.5 %collective-permute-start.11 = (f32[64,1024]{1,0:T(8,128)S(1)}, f32[64,1024]{1,0:T(8,128)S(1)}, u32[]{:S(2)}, u32[]{:S(2)}) collective-permute-start(f32[64,1024]{1,0:T(8,128)S(1)} %slice_select_fusion.2), channel_id=1, source_target_pairs={{0,4},{4,8},{8,12},{12,0},{1,5},{5,9},{9,13},{13,1},{2,6},{6,10},{... | collective-permute-start | bytes 786440 | tf_op jit(solution)/shard_map/ppermute | solution.py:163
  76.9 21.2 %collective-permute-start.15 = (f32[256,3584]{1,0:T(8,128)}, f32[256,3584]{1,0:T(8,128)}, u32[]{:S(2)}, u32[]{:S(2)}) collective-permute-start(f32[256,3584]{1,0:T(8,128)} %maximum_select_fusion.left_ref), channel_id=1, source_target_pairs={{0,1},{1,0},{2,3},{3,2},{4,5},{5,4},{6,7},{7,6},{8,9},{9,8},{10,11... | collective-permute-start | bytes 11010056 | tf_op jit(solution)/shard_map/ppermute | solution.py:148
  77.9 20.3 %collective-permute-start.14 = (f32[192,1024]{1,0:T(8,128)}, f32[192,1024]{1,0:T(8,128)}, u32[]{:S(2)}, u32[]{:S(2)}) collective-permute-start(f32[192,1024]{1,0:T(8,128)} %pad_maximum_fusion), channel_id=1, source_target_pairs={{0,16},{16,0},{1,17},{17,1},{2,18},{18,2},{3,19},{19,3},{4,20},{20... | collective-permute-start | bytes 2359304 | tf_op jit(solution)/shard_map/ppermute | solution.py:148
  100.3 9.7 %collective-permute-start.16 = (f32[48,3584]{1,0:T(8,128)}, f32[48,3584]{1,0:T(8,128)S(1)}, u32[]{:S(2)}, u32[]{:S(2)}) collective-permute-start(f32[48,3584]{1,0:T(8,128)} %slice_select_fusion.1), channel_id=1, source_target_pairs={{0,1},{1,0},{2,3},{3,2},{4,5},{5,4},{6,7},{7,6},{8,9},{9,8},{10,11... | collective-permute-start | bytes 2064392 | tf_op jit(solution)/shard_map/ppermute | solution.py:148
  101.1 7.5 %collective-permute-start.6 = (f32[48,1024]{1,0:T(8,128)}, f32[48,1024]{1,0:T(8,128)S(1)}, u32[]{:S(2)}, u32[]{:S(2)}) collective-permute-start(f32[48,1024]{1,0:T(8,128)} %slice_select_fusion.3), channel_id=1, source_target_pairs={{0,4},{4,0},{8,12},{12,8},{1,5},{5,1},{9,13},{13,9},{2,6},{6,2},{1... | collective-permute-start | bytes 589832 | tf_op jit(solution)/shard_map/ppermute | solution.py:180
  108.7 7.4 %collective-permute-start.7 = (f32[24,1024]{1,0:T(8,128)S(1)}, f32[24,1024]{1,0:T(8,128)S(1)}, u32[]{:S(2)}, u32[]{:S(2)}) collective-permute-start(f32[24,1024]{1,0:T(8,128)S(1)} %slice_select_fusion.4), channel_id=1, source_target_pairs={{0,8},{4,12},{8,0},{12,4},{1,9},{5,13},{9,1},{13,5},{2,10},{6,14},... | collective-permute-start | bytes 294920 | tf_op jit(solution)/shard_map/ppermute | solution.py:180
  110.1 16.9 %collective-permute-start.17 = (f32[48,3584]{1,0:T(8,128)S(1)}, f32[48,3584]{1,0:T(8,128)S(1)}, u32[]{:S(2)}, u32[]{:S(2)}) collective-permute-start(f32[48,3584]{1,0:T(8,128)S(1)} %select_add_fusion), channel_id=1, source_target_pairs={{0,2},{2,0},{1,3},{3,1},{4,6},{6,4},{5,7},{7,5},{8,10},{10,8},{9,1... | collective-permute-start | bytes 2064392 | tf_op jit(solution)/shard_map/ppermute | solution.py:148
  116.1 6.0 %collective-permute-start.8 = (f32[24,1024]{1,0:T(8,128)S(1)}, f32[24,1024]{1,0:T(8,128)S(1)}, u32[]{:S(2)}, u32[]{:S(2)}) collective-permute-start(f32[24,1024]{1,0:T(8,128)S(1)} %select_add_fusion.2), channel_id=1, source_target_pairs={{0,8},{4,12},{8,0},{12,4},{1,9},{5,13},{9,1},{13,5},{2,10},{6,14},... | collective-permute-start | bytes 294920 | tf_op jit(solution)/shard_map/ppermute | solution.py:180
  122.2 6.4 %collective-permute-start.9 = (f32[48,1024]{1,0:T(8,128)S(1)}, f32[48,1024]{1,0:T(8,128)S(1)}, u32[]{:S(2)}, u32[]{:S(2)}) collective-permute-start(f32[48,1024]{1,0:T(8,128)S(1)} %maximum_select_fusion.9), channel_id=1, source_target_pairs={{0,4},{4,0},{8,12},{12,8},{1,5},{5,1},{9,13},{13,9},{2,6},{6,2},{1... | collective-permute-start | bytes 589832 | tf_op jit(solution)/shard_map/ppermute | solution.py:180
  127.0 3.7 %collective-permute-start.18 = (f32[48,3584]{1,0:T(8,128)S(1)}, f32[48,3584]{1,0:T(8,128)S(1)}, u32[]{:S(2)}, u32[]{:S(2)}) collective-permute-start(f32[48,3584]{1,0:T(8,128)S(1)} %add.99), channel_id=1, source_target_pairs={{0,1},{1,0},{2,3},{3,2},{4,5},{5,4},{6,7},{7,6},{8,9},{9,8},{10,11... | collective-permute-start | bytes 2064392 | tf_op jit(solution)/shard_map/ppermute | solution.py:148
  196.3 5.6 %collective-permute-start.19 = (f32[4,128]{0,1:T(8,128)S(1)}, f32[4,128]{0,1:T(8,128)S(1)}, u32[]{:S(2)}, u32[]{:S(2)}) collective-permute-start(f32[4,128]{0,1:T(8,128)S(1)} %slice_select_fusion.5), channel_id=1, source_target_pairs={{0,8},{4,12},{8,0},{12,4},{1,9},{5,13},{9,1},{13,5},{2,10},{6,14},... | collective-permute-start | bytes 6152 | tf_op jit(solution)/shard_map/ppermute | solution.py:180
  202.0 4.0 %collective-permute-start.20 = (f32[4,64]{0,1:T(8,128)S(1)}, f32[4,64]{0,1:T(8,128)S(1)}, u32[]{:S(2)}, u32[]{:S(2)}) collective-permute-start(f32[4,64]{0,1:T(8,128)S(1)} %slice_select_fusion.6), channel_id=1, source_target_pairs={{0,4},{4,0},{8,12},{12,8},{1,5},{5,1},{9,13},{13,9},{2,6},{6,2},{1... | collective-permute-start | bytes 3080 | tf_op jit(solution)/shard_map/ppermute | solution.py:180
  206.0 3.8 %collective-permute-start.21 = (f32[4,32]{0,1:T(8,128)S(1)}, f32[4,32]{0,1:T(8,128)S(1)}, u32[]{:S(2)}, u32[]{:S(2)}) collective-permute-start(f32[4,32]{0,1:T(8,128)S(1)} %slice_select_fusion.7), channel_id=1, source_target_pairs={{0,2},{2,0},{1,3},{3,1},{4,6},{6,4},{5,7},{7,5},{8,10},{10,8},{9,1... | collective-permute-start | bytes 1544 | tf_op jit(solution)/shard_map/ppermute | solution.py:180
  209.8 1.2 collective-permute-start.22
  (9 other events, 52.2 us)
